TPU v7x, 32 devices: a whole 2x2x4 slice. The times are simulated.
32 devices in a mesh: groups: 2 (over x), mesh: 16 (over z, y, core).
Axes of the slice: x: 2, y: 2, z: 4, core: 2. Of those that a mesh axis runs over, the one named last changes fastest.
Arguments:
- node_feat: bfloat16 [32768, 256], P(('groups', 'mesh')), parts along dimension 0, may hold values from -6 to 6
- coarse_feat: bfloat16 [8192, 256], P(('groups', 'mesh')), parts along dimension 0, may hold values from -6 to 6
- neighbors: int32 [16384, 6], P('mesh'), may hold values from 0 to 16383, as said below
- up_owner: int32 [16384, 1], P('mesh'), may hold values from 0 to 15; in each aligned block of 1024 rows (0 to 1023, 1024 to 2047, ...) at most 128 rows name the same one
- up_local: int32 [16384], P('mesh'), may hold values from 0 to 255
- w_src: bfloat16 [2, 256, 256], replicated, may hold values from -0.375 to 0.375
- w_dst: bfloat16 [2, 256, 256], replicated, may hold values from -0.375 to 0.375
- w_node: bfloat16 [2, 256, 256], replicated, may hold values from -0.375 to 0.375
- w_edge: bfloat16 [2, 256, 256], replicated, may hold values from -0.15625 to 0.15625
- w_mix: bfloat16 [2, 256, 256], replicated, may hold values from -0.375 to 0.375
- edge_bias: float32 [2, 256], replicated, may hold values from -4 to 4
- w_up: bfloat16 [256, 256], replicated, may hold values from -0.375 to 0.375
- w_coarse: bfloat16 [256, 256], replicated, may hold values from -0.375 to 0.375
- w_down: bfloat16 [256, 256], replicated, may hold values from -0.375 to 0.375
Outputs:
- fine_out: bfloat16 [32768, 256], P(('groups', 'mesh')), parts along dimension 0
- coarse_out: bfloat16 [8192, 256], P(('groups', 'mesh')), parts along dimension 0
There are 2 independent parts, one for each index of `groups`. A program takes and returns all parts, laid end to end along the dimension named above; an argument that names none is the same for every part. Nothing has to cross between parts.
Inputs may be any that keep to these rules, and one draw needn't show every extreme that they name: `neighbors`: entry (i, k) is (i + o) modulo 16384 with o between -128 and 128 and never 0; the offsets 128 and -128 both occur. `up_owner`: among the 1024 rows of one device no owner is named more than 128 times, a bound that some block reaches.
All inputs are finite; a program needn't handle non-finite values.
Results may differ from a plain program's by a relative error of at most 0.0071.
Values may be sent and summed in bfloat16 or wider, within the bound.
A program may use at most 64 MiB of HBM per device.

v0:
```python
import jax
import jax.numpy as jnp
from jax import lax
from jax.sharding import PartitionSpec as P

R = 128
ROUNDS = 2


def extended(cells, sides, width):
    for axis, dim in sides:
        count = lax.axis_size(axis)
        head = lax.slice_in_dim(cells, 0, width, axis=dim)
        tail = lax.slice_in_dim(cells, cells.shape[dim] - width, cells.shape[dim], axis=dim)
        cells = jnp.concatenate(
            [
                lax.ppermute(tail, axis, [(i, (i + 1) % count) for i in range(count)]),
                cells,
                lax.ppermute(head, axis, [((i + 1) % count, i) for i in range(count)]),
            ],
            axis=dim,
        )
    return cells


def shards(
    node_feat,
    coarse_feat,
    neighbors,
    up_owner,
    up_local,
    w_src,
    w_dst,
    w_node,
    w_edge,
    w_mix,
    edge_bias,
    w_up,
    w_coarse,
    w_down,
):
    row_count = node_feat.shape[0]
    width = node_feat.shape[1]
    edge_count = neighbors.shape[1]
    peer_count = lax.axis_size("mesh")
    my_index = lax.axis_index("mesh")
    overall_row_count = row_count * peer_count
    first_own = my_index * row_count
    local_index = jnp.mod(neighbors - first_own + R, overall_row_count)
    block_rows = min(128, row_count)
    number_of_blocks = row_count // block_rows
    window_rows = block_rows + 2 * R
    window_iota = jnp.arange(window_rows, dtype=jnp.int32)
    index_blocks = local_index.reshape(number_of_blocks, block_rows, edge_count)
    hidden_width = node_feat
    for round_index in range(ROUNDS):
        src_term = jnp.dot(hidden_width, w_src[round_index], preferred_element_type=jnp.float32)
        dst_term = jnp.dot(
            hidden_width, w_dst[round_index], preferred_element_type=jnp.float32
        ).astype(jnp.bfloat16)
        padded = extended(dst_term, (("mesh", 0),), R)
        biased = src_term + edge_bias[round_index][None, :]

        def edge_block(inputs):
            block_id, index_block, biased_block = inputs
            block_start = block_id * block_rows
            window_span = lax.dynamic_slice_in_dim(padded, block_start, window_rows, 0)
            relative_index = index_block - block_start
            indicator_matrix = (relative_index[:, :, None] == window_iota[None, None, :]).astype(
                jnp.bfloat16
            )
            selected_rows = jnp.einsum(
                "cai,iy->cay", indicator_matrix, window_span, preferred_element_type=jnp.float32
            )
            return jnp.sum(jax.nn.silu(biased_block[:, None, :] + selected_rows), axis=1)

        edge_sum = lax.map(
            edge_block,
            (
                jnp.arange(number_of_blocks, dtype=jnp.int32),
                index_blocks,
                biased.reshape(number_of_blocks, block_rows, width),
            ),
        ).reshape(row_count, width)
        node_update = jax.nn.silu(
            jnp.dot(hidden_width, w_node[round_index], preferred_element_type=jnp.float32)
            + jnp.dot(
                edge_sum.astype(jnp.bfloat16),
                w_edge[round_index],
                preferred_element_type=jnp.float32,
            )
        ).astype(jnp.bfloat16)
        hidden_width = (
            hidden_width.astype(jnp.float32)
            + jnp.dot(node_update, w_mix[round_index], preferred_element_type=jnp.float32)
        ).astype(jnp.bfloat16)
    message = jax.nn.silu(jnp.dot(hidden_width, w_up, preferred_element_type=jnp.float32)).astype(
        jnp.bfloat16
    )
    owner_of = up_owner[:, 0]
    coarse_count = coarse_feat.shape[0]
    slot_capacity = 2 * row_count // peer_count
    slot_total = peer_count * slot_capacity
    owner_hot = (owner_of[:, None] == jnp.arange(peer_count, dtype=jnp.int32)[None, :]).astype(
        jnp.bfloat16
    )
    row_iota = jnp.arange(row_count, dtype=jnp.int32)
    lower = (row_iota[:, None] >= row_iota[None, :]).astype(jnp.bfloat16)
    inclusive = jnp.dot(lower, owner_hot, preferred_element_type=jnp.float32)
    slot_rank = (jnp.sum(inclusive * owner_hot.astype(jnp.float32), axis=1) - 1.0).astype(jnp.int32)
    slot_of = owner_of * slot_capacity + slot_rank
    slot_iota = jnp.arange(slot_total, dtype=jnp.int32)
    slot_match = slot_iota[:, None] == slot_of[None, :]
    slot_select = slot_match.astype(jnp.bfloat16)
    outbox = jnp.dot(slot_select, message, preferred_element_type=jnp.float32).astype(jnp.bfloat16)
    outbox_index = jnp.sum(jnp.where(slot_match, up_local[None, :] + 1, 0), axis=1) - 1
    inbox, inbox_index = (
        lax.all_to_all(
            outbox.reshape(peer_count, slot_capacity, width),
            "mesh",
            split_axis=0,
            concat_axis=0,
            tiled=True,
        ),
        lax.all_to_all(
            outbox_index.reshape(peer_count, slot_capacity),
            "mesh",
            split_axis=0,
            concat_axis=0,
            tiled=True,
        ),
    )
    inbox_rows = inbox.reshape(slot_total, width)
    flat_index = inbox_index.reshape(slot_total)
    coarse_iota = jnp.arange(coarse_count, dtype=jnp.int32)
    coarse_select = (coarse_iota[:, None] == flat_index[None, :]).astype(jnp.bfloat16)
    summed = jnp.dot(coarse_select, inbox_rows, preferred_element_type=jnp.float32)
    child_count = jnp.sum(coarse_select.astype(jnp.float32), axis=1)
    coarse_mean = (summed / jnp.maximum(child_count, 1.0)[:, None]).astype(jnp.bfloat16)
    coarse_out = (
        coarse_feat.astype(jnp.float32)
        + jnp.dot(coarse_mean, w_coarse, preferred_element_type=jnp.float32)
    ).astype(jnp.bfloat16)
    reply_select = (flat_index[:, None] == coarse_iota[None, :]).astype(jnp.bfloat16)
    replies = jnp.dot(reply_select, coarse_out, preferred_element_type=jnp.float32).astype(
        jnp.bfloat16
    )
    returned = lax.all_to_all(
        replies.reshape(peer_count, slot_capacity, width),
        "mesh",
        split_axis=0,
        concat_axis=0,
        tiled=True,
    )
    parent_feat = jnp.einsum(
        "sf,sd->fd",
        slot_select,
        returned.reshape(slot_total, width),
        preferred_element_type=jnp.float32,
    ).astype(jnp.bfloat16)
    fine_out = (
        hidden_width.astype(jnp.float32)
        + jnp.dot(parent_feat, w_down, preferred_element_type=jnp.float32)
    ).astype(jnp.bfloat16)
    return (fine_out, coarse_out)


def solution(mesh):
    in_specs = (
        P(("groups", "mesh"), None),
        P(("groups", "mesh"), None),
        P("mesh", None),
        P("mesh", None),
        P("mesh"),
        P(),
        P(),
        P(),
        P(),
        P(),
        P(),
        P(),
        P(),
        P(),
    )
    out_specs = (P(("groups", "mesh"), None), P(("groups", "mesh"), None))
    return jax.shard_map(shards, mesh=mesh, in_specs=in_specs, out_specs=out_specs, check_vma=False)
```

profile of v0, /device:TPU:1, one launch (start us, length us, event | category | flops | bytes accessed | tf_op | source)
XLA Modules:
  0.0 157.4 jit_solution(18030434749348789217)
XLA Ops:
  0.7 1.4 convolution_convert_fusion.2
  2.8 2.6 %collective-permute-start = (bf16[128,256]{1,0:T(8,128)(2,1)}, bf16[128,256]{1,0:T(8,128)(2,1)}, u32[]{:S(2)}, u32[]{:S(2)}) collective-permute-start(bf16[128,256]{1,0:T(8,128)(2,1)} %get-tuple-element.132), channel_id=1, source_target_pairs={{0,1},{1,2},{2,3},{3,4},{4,5},{5,6},{6,7},{7,8},{8,9},{9,10},{10,1... | collective-permute-start | bytes 196616 | tf_op jit(solution)/shard_map/ppermute | solution.py:17
  5.9 0.9 select_reduce_fusion
  7.5 6.5 %all-to-all-start = ((s32[16,1,128]{2,1,0:T(1,128)}), s32[16,1,128]{2,1,0:T(1,128)S(1)}, u32[]{:S(2)}, u32[]{:S(2)}) async-start(s32[16,1,128]{2,1,0:T(1,128)} %bitcast.18), calls=%async_computation | async-start | bytes 16384 | tf_op jit(solution)/shard_map/all_to_all | solution.py:125
  14.6 1.4 fusion.64
  16.0 1.8 %pad_maximum_fusion = bf16[1280,256]{1,0:T(8,128)(2,1)} fusion(bf16[128,256]{1,0:T(8,128)(2,1)} %collective-permute-done.1, bf16[1024,256]{1,0:T(8,128)(2,1)S(1)} %convolution_convert_fusion.2, bf16[128,256]{1,0:T(8,128)(2,1)} %collective-permute-done), kind=kLoop, calls=%fused_computation.61 | loop fusion | flops 1966080 | bytes 1310720 | tf_op jit(solution)/shard_map/concatenate | solution.py:15
  17.7 0.8 broadcast.60.clone
  18.6 32.0 %while.22 = (s32[]{:T(128)}, bf16[8,128,256]{2,1,0:T(8,128)(2,1)}, f32[8,128,256]{2,1,0:T(8,128)S(1)}, s32[8,128,6]{1,2,0:T(8,128)}, s32[8]{0:T(128)S(1)}, /*ind...) while((s32[]{:T(128)}, bf16[8,128,256]{2,1,0:T(8,128)(2,1)}, ...), condition=%wide.region_2.3_spmd.clone, body=%wide.region_0.2_spmd.clone.sunk | while | flops 152437504 | bytes 796335 | solution.py:77
  20.5 1.4 multiply_reduce_fusion.4
  23.8 0.7 subtract_bitcast_fusion.4
  24.5 1.4 multiply_reduce_fusion.4
  27.8 0.7 subtract_bitcast_fusion.4
  28.5 1.4 multiply_reduce_fusion.4
  31.8 0.7 subtract_bitcast_fusion.4
  32.5 1.4 multiply_reduce_fusion.4
  35.8 0.7 subtract_bitcast_fusion.4
  36.5 1.4 multiply_reduce_fusion.4
  40.5 1.4 multiply_reduce_fusion.4
  43.8 0.7 subtract_bitcast_fusion.4
  44.5 1.4 multiply_reduce_fusion.4
  47.8 0.7 subtract_bitcast_fusion.4
  48.5 1.4 multiply_reduce_fusion.4
  50.6 1.7 %fusion.20 = bf16[1024,256]{1,0:T(8,128)(2,1)S(1)} fusion(f32[1024,256]{1,0:T(8,128)S(1)} %fusion.47, bf16[1024,256]{1,0:T(8,128)(2,1)} %bitcast.6, bf16[1024,256]{1,0:T(8,128)(2,1)S(1)} %copy-done.1, bf16[2,256,256]{2,1,0:T(8,128)(2,1)} %param.27, bf16[2,256,256]{2,1,0:T(8,128)(2,1)} %param.26), kind=kOutput, calls=%fused_computation.46 | convolution fusion | flops 270794752 | bytes 2883584 | tf_op jit(solution)/shard_map/dot_general | solution.py:95
  52.6 1.7 %collective-permute-start.2 = (bf16[128,256]{1,0:T(8,128)(2,1)S(1)}, bf16[128,256]{1,0:T(8,128)(2,1)S(1)}, u32[]{:S(2)}, u32[]{:S(2)}) collective-permute-start(bf16[128,256]{1,0:T(8,128)(2,1)S(1)} %get-tuple-element.130), channel_id=1, source_target_pairs={{0,1},{1,2},{2,3},{3,4},{4,5},{5,6},{6,7},{7,8},{8,9},{9,10},{10,1... | collective-permute-start | bytes 196616 | tf_op jit(solution)/shard_map/ppermute | solution.py:17
  54.9 0.7 collective-permute-done.2
  55.7 3.1 %collective-permute-done.3 = bf16[128,256]{1,0:T(8,128)(2,1)S(1)} collective-permute-done((bf16[128,256]{1,0:T(8,128)(2,1)S(1)}, bf16[128,256]{1,0:T(8,128)(2,1)S(1)}, u32[]{:S(2)}, u32[]{:S(2)}) %collective-permute-start.3) | collective-permute-done | bytes 65568 | tf_op jit(solution)/shard_map/ppermute | solution.py:19
  58.8 0.9 pad_maximum_fusion.1
  59.7 27.2 %while.23 = (s32[]{:T(128)}, bf16[8,128,256]{2,1,0:T(8,128)(2,1)S(1)}, f32[8,128,256]{2,1,0:T(8,128)S(1)}, s32[8,128,6]{1,2,0:T(8,128)}, s32[8]{0:T(128)S(1)}, /...) while((s32[]{:T(128)}, bf16[8,128,256]{2,1,0:T(8,128)(2,1)S(1)}, ...), condition=%wide.region_5.6_spmd.clone, body=%wide.region_3.5_spmd.clone.sunk | while | flops 152437504 | bytes 795827 | solution.py:77
  61.7 1.4 multiply_reduce_fusion.5
  64.4 0.7 subtract_bitcast_fusion.5
  65.1 1.4 multiply_reduce_fusion.5
  67.8 0.7 subtract_bitcast_fusion.5
  68.5 1.4 multiply_reduce_fusion.5
  71.2 0.7 subtract_bitcast_fusion.5
  71.9 1.4 multiply_reduce_fusion.5
  75.3 1.4 multiply_reduce_fusion.5
  78.7 1.4 multiply_reduce_fusion.5
  81.4 0.7 subtract_bitcast_fusion.5
  82.1 1.4 multiply_reduce_fusion.5
  84.8 0.7 subtract_bitcast_fusion.5
  85.5 1.4 multiply_reduce_fusion.5
  86.9 1.5 fusion.21
  88.5 3.0 %fusion.17 = bf16[2048,256]{1,0:T(8,128)(2,1)} fusion(s32[1024]{0:T(1024)S(1)} %copy-done.9, bf16[1024,256]{1,0:T(8,128)(2,1)S(1)} %fusion.21, bf16[256,256]{1,0:T(8,128)(2,1)S(1)} %copy-done), kind=kOutput, calls=%fused_computation.30 | convolution fusion | flops 1211891712 | bytes 1708032 | tf_op jit(solution)/shard_map/dot_general | solution.py:115
  91.5 6.2 %all-to-all-start.1 = ((bf16[16,128,256]{2,1,0:T(8,128)(2,1)}), bf16[16,128,256]{2,1,0:T(8,128)(2,1)S(1)}, u32[]{:S(2)}, u32[]{:S(2)}) async-start(bf16[16,128,256]{2,1,0:T(8,128)(2,1)} %bitcast.20), calls=%async_computation.1 | async-start | bytes 2097152 | tf_op jit(solution)/shard_map/all_to_all | solution.py:118
  98.1 22.8 %all-to-all-done.1 = bf16[16,128,256]{2,1,0:T(8,128)(2,1)S(1)} async-done(((bf16[16,128,256]{2,1,0:T(8,128)(2,1)}), bf16[16,128,256]{2,1,0:T(8,128)(2,1)S(1)}, u32[]{:S(2)}, u32[]{:S(2)}) %all-to-all-start.1) | async-done | bytes 1048608 | tf_op jit(solution)/shard_map/all_to_all | solution.py:118
  121.5 0.7 convolution_convert_fusion
  122.3 31.8 %all_to_all.16 = bf16[16,128,256]{2,1,0:T(8,128)(2,1)S(1)} all-to-all(bf16[16,128,256]{2,1,0:T(8,128)(2,1)S(1)} %bitcast.106), channel_id=1, replica_groups=mesh['groups'=2,'mesh'=16] {'mesh'}, dimensions={0} | all-to-all | bytes 2097152 | tf_op jit(solution)/shard_map/all_to_all | solution.py:148
  154.1 3.3 %fusion.22 = bf16[1024,256]{1,0:T(8,128)(2,1)} fusion(bf16[256,256]{1,0:T(8,128)(2,1)S(1)} %copy-done.13, bf16[2048,256]{1,0:T(8,128)(2,1)S(1)} %bitcast.105, s32[1024]{0:T(1024)S(1)} %copy-done.9, bf16[1024,256]{1,0:T(8,128)(2,1)S(1)} %fusion.21), kind=kOutput, calls=%fused_computation.48 | convolution fusion | flops 1211105280 | bytes 2232320 | tf_op jit(solution)/shard_map/dot_general | solution.py:163
  (105 shorter events, 22.4 us)
Async XLA Ops:
  0.6 87.9 %copy-start = (bf16[256,256]{1,0:T(8,128)(2,1)S(1)}, bf16[256,256]{1,0:T(8,128)(2,1)}, u32[]{:S(2)}) copy-start(bf16[256,256]{1,0:T(8,128)(2,1)} %param.29) | copy-start | bytes 393220
  0.6 4.7 %copy-start.6 = (s32[1024,1]{0,1:T(1,128)S(1)}, s32[1024,1]{0,1:T(1,128)}, u32[]{:S(2)}) copy-start(s32[1024,1]{0,1:T(1,128)} %param.21) | copy-start | bytes 12292
  0.7 5.2 %copy-start.7 = (s32[1024]{0:T(1024)S(1)}, s32[1024]{0:T(1024)}, u32[]{:S(2)}) copy-start(s32[1024]{0:T(1024)} %param.22) | copy-start | bytes 12292
  2.1 11.9 %copy-start.10 = (f32[2,256]{1,0:T(2,128)S(1)}, f32[2,256]{1,0:T(2,128)}, u32[]{:S(2)}) copy-start(f32[2,256]{1,0:T(2,128)} %param.28) | copy-start | bytes 6148
  2.1 11.9 %copy-start.1 = (bf16[1024,256]{1,0:T(8,128)(2,1)S(1)}, bf16[1024,256]{1,0:T(8,128)(2,1)}, u32[]{:S(2)}) copy-start(bf16[1024,256]{1,0:T(8,128)(2,1)} %param.18) | copy-start | bytes 1572868
  2.1 11.9 %copy-start.4 = (bf16[2,256,256]{2,1,0:T(8,128)(2,1)S(1)}, bf16[2,256,256]{2,1,0:T(8,128)(2,1)}, u32[]{:S(2)}) copy-start(bf16[2,256,256]{2,1,0:T(8,128)(2,1)} %param.25) | copy-start | bytes 786436
  2.8 13.2 %collective-permute-start = (bf16[128,256]{1,0:T(8,128)(2,1)}, bf16[128,256]{1,0:T(8,128)(2,1)}, u32[]{:S(2)}, u32[]{:S(2)}) collective-permute-start(bf16[128,256]{1,0:T(8,128)(2,1)} %get-tuple-element.132), channel_id=1, source_target_pairs={{0,1},{1,2},{2,3},{3,4},{4,5},{5,6},{6,7},{7,8},{8,9},{9,10},{10,1... | collective-permute-start | bytes 196616 | tf_op jit(solution)/shard_map/ppermute | solution.py:17
  5.4 10.6 %collective-permute-start.1 = (bf16[128,256]{1,0:T(8,128)(2,1)}, bf16[128,256]{1,0:T(8,128)(2,1)}, u32[]{:S(2)}, u32[]{:S(2)}) collective-permute-start(bf16[128,256]{1,0:T(8,128)(2,1)} %get-tuple-element.133), channel_id=1, source_target_pairs={{1,0},{2,1},{3,2},{4,3},{5,4},{6,5},{7,6},{8,7},{9,8},{10,9},{11,1... | collective-permute-start | bytes 196616 | tf_op jit(solution)/shard_map/ppermute | solution.py:19
  5.9 8.4 %copy-start.3 = (bf16[2,256,256]{2,1,0:T(8,128)(2,1)S(1)}, bf16[2,256,256]{2,1,0:T(8,128)(2,1)}, u32[]{:S(2)}) copy-start(bf16[2,256,256]{2,1,0:T(8,128)(2,1)} %param.23) | copy-start | bytes 786436
  5.9 8.0 %copy-start.8 = (s32[1024]{0:T(1024)}, s32[1024]{0:T(1024)S(1)}, u32[]{:S(2)}) copy-start(s32[1024]{0:T(1024)S(1)} %get-tuple-element.136) | copy-start | bytes 12292
  7.5 84.1 %all-to-all-start = ((s32[16,1,128]{2,1,0:T(1,128)}), s32[16,1,128]{2,1,0:T(1,128)S(1)}, u32[]{:S(2)}, u32[]{:S(2)}) async-start(s32[16,1,128]{2,1,0:T(1,128)} %bitcast.18), calls=%async_computation | async-start | bytes 16384 | tf_op jit(solution)/shard_map/all_to_all | solution.py:125
  50.6 1.7 %copy-start.2 = (bf16[2,256,256]{2,1,0:T(8,128)(2,1)S(1)}, bf16[2,256,256]{2,1,0:T(8,128)(2,1)}, u32[]{:S(2)}) copy-start(bf16[2,256,256]{2,1,0:T(8,128)(2,1)} %param.24) | copy-start | bytes 786436
  52.6 2.0 %copy-start.5 = (bf16[2,256,256]{2,1,0:T(8,128)(2,1)S(1)}, bf16[2,256,256]{2,1,0:T(8,128)(2,1)}, u32[]{:S(2)}) copy-start(bf16[2,256,256]{2,1,0:T(8,128)(2,1)} %param.25) | copy-start | bytes 786436
  52.6 3.0 %collective-permute-start.2 = (bf16[128,256]{1,0:T(8,128)(2,1)S(1)}, bf16[128,256]{1,0:T(8,128)(2,1)S(1)}, u32[]{:S(2)}, u32[]{:S(2)}) collective-permute-start(bf16[128,256]{1,0:T(8,128)(2,1)S(1)} %get-tuple-element.130), channel_id=1, source_target_pairs={{0,1},{1,2},{2,3},{3,4},{4,5},{5,6},{6,7},{7,8},{8,9},{9,10},{10,1... | collective-permute-start | bytes 196616 | tf_op jit(solution)/shard_map/ppermute | solution.py:17
  54.3 4.5 %collective-permute-start.3 = (bf16[128,256]{1,0:T(8,128)(2,1)S(1)}, bf16[128,256]{1,0:T(8,128)(2,1)S(1)}, u32[]{:S(2)}, u32[]{:S(2)}) collective-permute-start(bf16[128,256]{1,0:T(8,128)(2,1)S(1)} %get-tuple-element.131), channel_id=1, source_target_pairs={{1,0},{2,1},{3,2},{4,3},{5,4},{6,5},{7,6},{8,7},{9,8},{10,9},{11,1... | collective-permute-start | bytes 196616 | tf_op jit(solution)/shard_map/ppermute | solution.py:19
  86.9 1.6 copy-start.9
  91.5 29.4 %copy-start.11 = (bf16[256,256]{1,0:T(8,128)(2,1)S(1)}, bf16[256,256]{1,0:T(8,128)(2,1)}, u32[]{:S(2)}) copy-start(bf16[256,256]{1,0:T(8,128)(2,1)} %param.30) | copy-start | bytes 393220
  91.5 29.4 %copy-start.12 = (bf16[256,256]{1,0:T(8,128)(2,1)S(1)}, bf16[256,256]{1,0:T(8,128)(2,1)}, u32[]{:S(2)}) copy-start(bf16[256,256]{1,0:T(8,128)(2,1)} %param.19) | copy-start | bytes 393220
  91.5 29.4 %all-to-all-start.1 = ((bf16[16,128,256]{2,1,0:T(8,128)(2,1)}), bf16[16,128,256]{2,1,0:T(8,128)(2,1)S(1)}, u32[]{:S(2)}, u32[]{:S(2)}) async-start(bf16[16,128,256]{2,1,0:T(8,128)(2,1)} %bitcast.20), calls=%async_computation.1 | async-start | bytes 2097152 | tf_op jit(solution)/shard_map/all_to_all | solution.py:118
  121.5 32.6 %copy-start.14 = (bf16[256,256]{1,0:T(8,128)(2,1)}, bf16[256,256]{1,0:T(8,128)(2,1)S(1)}, u32[]{:S(2)}) copy-start(bf16[256,256]{1,0:T(8,128)(2,1)S(1)} %fusion.25) | copy-start | bytes 393220
  122.3 31.8 %copy-start.13 = (bf16[256,256]{1,0:T(8,128)(2,1)S(1)}, bf16[256,256]{1,0:T(8,128)(2,1)}, u32[]{:S(2)}) copy-start(bf16[256,256]{1,0:T(8,128)(2,1)} %param.31) | copy-start | bytes 393220
where the time goes:
time: 159 us; the launch traced here: 157 us
  matrix products  36.9 us (23%)
  blocking collectives  31.8 us (20%)
  waiting for transfers between devices  26.7 us (17%)
  starting transfers between devices  17 us (11%)
  other arithmetic  16.8 us (11%)
  local copies, waits for them, and re-layouts  16.3 us (10%)
  loops' own time  10.9 us (7%)
    all_to_all x1, blocking collectives, shards(): lax.all_to_all(replies.reshape(peer_count, slot_capacity, width), 'mesh',...  31.8 us
    all_to_all x1, waiting for transfers between devices, shards(): lax.all_to_all(outbox.reshape(peer_count, slot_capacity, width), 'mesh',...  22.8 us
    dot_general x16, matrix products, edge_block(): jnp.einsum('cai,iy->cay', indicator_matrix, window_span, preferred_elemen...  22.6 us
    sub x16, other arithmetic, edge_block(): relative_index = index_block - block_start  11 us
    another operation x2, loops' own time, shards(): lax.map(edge_block, (jnp.arange(number_of_blocks, dtype=jnp.int32), index...  10.9 us
    dynamic_slice x16, local copies, waits for them, and re-layouts, shards(): lax.map(edge_block, (jnp.arange(number_of_blocks, dtype=jnp.int32), index...  9.35 us
    all_to_all x1, starting transfers between devices, shards(): lax.all_to_all(outbox_index.reshape(peer_count, slot_capacity), 'mesh', s...  6.46 us
    all_to_all x1, starting transfers between devices, shards(): lax.all_to_all(outbox.reshape(peer_count, slot_capacity, width), 'mesh',...  6.22 us
  transfers between devices with their start and end apart: 6, of which 3 were waited for; matrix products, arithmetic and copies ran while one was open for 40% of the time, Pallas kernels for 0%

commit v1 on v0

v1 whole, which is shorter than its diff:
```python
import functools

import jax
import jax.numpy as jnp
from jax import lax
from jax.experimental import pallas as pl
from jax.experimental.pallas import tpu as pltpu
from jax.sharding import PartitionSpec as P

R = 128
ROUNDS = 2
BLOCK = 128
BF = jnp.bfloat16
F32 = jnp.float32


def dot(a, b):
    return jnp.dot(a, b, preferred_element_type=F32)


def silu(x):
    h = 0.5 * x
    return h + h * jnp.tanh(h)


def kernel(
    n,
    x_ref,
    cf_ref,
    nb_ref,
    pc_ref,
    pr_ref,
    w_src,
    w_dst,
    w_node,
    w_edge,
    w_mix,
    bias_ref,
    w_up,
    w_coarse,
    w_down,
    fine_ref,
    coarse_ref,
    pick,
    ext,
    srch,
    esum,
    hid,
    msg,
    sib_row,
    hist,
    counts,
    sbuf,
    rbuf,
    gath,
    acc,
    halo_s,
    halo_r,
    cnt_s,
    cnt_r,
    row_s,
    row_r,
    msg_s,
    msg_r,
    red_s,
    red_r,
    ag_s,
    ag_r,
    sib_s,
    sib_r,
):
    rows, width = x_ref.shape
    edges = nb_ref.shape[1]
    cells = cf_ref.shape[0]
    half = cells // 2
    blocks = rows // BLOCK
    window = BLOCK + 2 * R
    ring = n // 2
    total = rows * n
    me = lax.axis_index("mesh")
    core = me % 2
    sibling = me + 1 - 2 * core
    chip = me // 2
    span = ring // 2
    pos = jnp.where(chip % 2 == 0, chip // 2, ring - 1 - chip // 2)

    def owner_at(place):
        place = (place + 2 * ring) % ring
        return jnp.where(place < span, 2 * place, 2 * (ring - 1 - place) + 1) * 2

    right = owner_at(pos + 1) + core
    left = owner_at(pos - 1) + core
    after = (me + 1) % n
    before = (me + n - 1) % n

    def remote(src, dst, ssem, rsem, dev):
        return pltpu.make_async_remote_copy(
            src_ref=src,
            dst_ref=dst,
            send_sem=ssem,
            recv_sem=rsem,
            device_id={"mesh": dev},
            device_id_type=pl.DeviceIdType.MESH,
        )

    barrier = pltpu.get_barrier_semaphore()

    def greet(j, c):
        pl.semaphore_signal(
            barrier,
            inc=1,
            device_id={"mesh": (me + j) % n},
            device_id_type=pl.DeviceIdType.MESH,
        )
        return c

    lax.fori_loop(1, n, greet, 0)

    ext[0, pl.ds(R, rows), :] = dot(x_ref[...], w_dst[0]).astype(BF)
    lows = (lax.broadcasted_iota(jnp.int32, (8 * n, 1), 0) // 8) * cells
    parents = pr_ref[...]
    owner_hot = jnp.where((parents >= lows) & (parents < lows + cells), 1.0, 0.0).astype(BF)
    local = jnp.bitwise_and(pc_ref[...], cells - 1)
    local_hot = jnp.where(
        local == lax.broadcasted_iota(jnp.int32, (rows, cells), 1), 1.0, 0.0
    ).astype(BF)
    hist[...] = dot(owner_hot, local_hot)

    pl.semaphore_wait(barrier, n - 1)

    def halo(l):
        return (
            remote(
                ext.at[l, pl.ds(R, R)],
                ext.at[l, pl.ds(R + rows, R)],
                halo_s.at[l, 0],
                halo_r.at[l, 0],
                before,
            ),
            remote(
                ext.at[l, pl.ds(rows, R)],
                ext.at[l, pl.ds(0, R)],
                halo_s.at[l, 1],
                halo_r.at[l, 1],
                after,
            ),
        )

    for c in halo(0):
        c.start()
    row_copy = remote(pr_ref, sib_row, row_s, row_r, sibling)
    row_copy.start()

    def count_copy(peer, slot):
        return remote(
            hist.at[pl.ds(peer * 8, 8)],
            counts.at[pl.ds(slot * 8, 8)],
            cnt_s.at[peer],
            cnt_r.at[slot],
            peer,
        )

    def send_counts(j, c):
        count_copy((me + j) % n, me).start()
        return c

    lax.fori_loop(1, n, send_counts, 0)

    def build(b, c):
        r0 = b * BLOCK
        rel = nb_ref[pl.ds(r0, BLOCK), :] - (me * rows - R)
        rel = jnp.where(rel < 0, rel + total, rel)
        rel = jnp.where(rel >= total, rel - total, rel) - r0
        lanes = lax.broadcasted_iota(jnp.int32, (BLOCK, window), 1)
        for k in range(edges):
            pick[b, pl.ds(k * BLOCK, BLOCK), :] = jnp.where(
                rel[:, k : k + 1] == lanes, 0.5, 0.0
            ).astype(BF)
        return c

    def edge_block(l, b):
        r0 = b * BLOCK
        if l == 0:
            build(b, 0)
        sel = dot(pick[b], ext[l, pl.ds(r0, window), :])
        base = srch[pl.ds(r0, BLOCK), :]
        out = jnp.zeros((BLOCK, width), F32)
        for k in range(edges):
            h = base + sel[k * BLOCK : (k + 1) * BLOCK]
            out = out + (h + h * jnp.tanh(h))
        esum[pl.ds(r0, BLOCK), :] = out.astype(BF)

    chunk = rows // 4

    def msg_copy(i):
        part = pl.ds(i * chunk, chunk)
        return remote(msg.at[0, part], msg.at[1, part], msg_s.at[i], msg_r.at[i], sibling)

    for l in range(ROUNDS):
        here = x_ref if l == 0 else hid
        srch[...] = 0.5 * (dot(here[...], w_src[l]) + bias_ref[l : l + 1, :])

        def inner(b, c, l=l):
            edge_block(l, b)
            return c

        lax.fori_loop(1, blocks - 1, inner, 0)
        for c in halo(l):
            c.wait_recv()

        def outer(j, c, l=l):
            edge_block(l, j * (blocks - 1))
            return c

        lax.fori_loop(0, 2, outer, 0)
        for i in range(4):
            part = pl.ds(i * chunk, chunk)
            old = here[part, :]
            upd = silu(dot(old, w_node[l]) + dot(esum[part, :], w_edge[l])).astype(BF)
            new = (old.astype(F32) + dot(upd, w_mix[l])).astype(BF)
            hid[part, :] = new
            if l + 1 < ROUNDS:
                ext[l + 1, pl.ds(R + i * chunk, chunk), :] = dot(new, w_dst[l + 1]).astype(BF)
            else:
                msg[0, part, :] = silu(dot(new, w_up[...])).astype(BF)
                msg_copy(i).start()
        if l + 1 < ROUNDS:
            for c in halo(l + 1):
                c.start()

    counts[pl.ds(pl.multiple_of(me * 8, 8), 8), :] = hist[pl.ds(pl.multiple_of(me * 8, 8), 8), :]

    def take_counts(j, c):
        count_copy(me, (me + j) % n).wait_recv()
        return c

    lax.fori_loop(1, n, take_counts, 0)
    number = jnp.zeros((8, cells), F32)
    for j in range(n):
        number = number + counts[j * 8 : (j + 1) * 8, :]
    diag = lax.broadcasted_iota(jnp.int32, (cells, cells), 0) == lax.broadcasted_iota(
        jnp.int32, (cells, cells), 1
    )
    number = jnp.sum(jnp.where(diag, number[0:1, :], 0.0), axis=1, keepdims=True)
    scale = 1.0 / jnp.maximum(number, 1.0)

    row_copy.wait_recv()
    for i in range(4):
        msg_copy(i).wait_recv()

    cell_iota = lax.broadcasted_iota(jnp.int32, (cells, 1), 0)

    def partial_sums(s):
        low = (owner_at(pos - 1 - s) + core) * cells
        high = (owner_at(pos + 1 + s) + core) * cells
        ids = cell_iota + jnp.where(cell_iota < half, low, high)
        mine = jnp.where(pr_ref[...] == ids, 1.0, 0.0).astype(BF)
        theirs = jnp.where(sib_row[...] == ids, 1.0, 0.0).astype(BF)
        return dot(mine, msg[0]) + dot(theirs, msg[1])

    def red_copy(d, s):
        return remote(
            sbuf.at[s, d],
            rbuf.at[s, d],
            red_s.at[s, d],
            red_r.at[s, d],
            right if d == 0 else left,
        )

    first = partial_sums(0)
    for d in range(2):
        sbuf[0, d] = first[d * half : (d + 1) * half].astype(BF)
        red_copy(d, 0).start()

    def reduce_step(s, c):
        part = partial_sums(s)
        for d in range(2):
            red_copy(d, s - 1).wait_recv()
            sbuf[s, d] = (
                part[d * half : (d + 1) * half] + rbuf[s - 1, d].astype(F32)
            ).astype(BF)
            red_copy(d, s).start()
        return c

    lax.fori_loop(1, ring - 1, reduce_step, 0)
    part = partial_sums(ring - 1)
    for d in range(2):
        red_copy(d, ring - 2).wait_recv()
        side = slice(d * half, (d + 1) * half)
        summed = part[side] + rbuf[ring - 2, d].astype(F32)
        mean = (summed * scale[side]).astype(BF)
        out = (cf_ref[side, :].astype(F32) + dot(mean, w_coarse[...])).astype(BF)
        coarse_ref[side, :] = out
        gath[0, 0, d] = out

    def ag_copy(d, s):
        return remote(
            gath.at[0, s, d],
            gath.at[0, s + 1, d],
            ag_s.at[s, d],
            ag_r.at[s, d],
            right if d == 0 else left,
        )

    def sib_copy(s):
        return remote(gath.at[0, s], gath.at[1, s], sib_s.at[s], sib_r.at[s], sibling)

    lane_iota = lax.broadcasted_iota(jnp.int32, (1, cells), 1)

    def gather(s):
        low = owner_at(pos - s)
        high = owner_at(pos + s)
        ids = lane_iota + jnp.where(lane_iota < half, low, high) * cells
        mine = ids + core * cells
        theirs = ids + (1 - core) * cells
        column = pc_ref[...]
        hot = jnp.where(column == mine, 1.0, 0.0).astype(BF)
        got = dot(hot, gath[0, s].reshape(cells, width))
        sib_copy(s).wait_recv()
        hot = jnp.where(column == theirs, 1.0, 0.0).astype(BF)
        return got + dot(hot, gath[1, s].reshape(cells, width))

    for d in range(2):
        ag_copy(d, 0).start()
    sib_copy(0).start()
    acc[...] = gather(0)

    def gather_step(s, c):
        for d in range(2):
            ag_copy(d, s - 1).wait_recv()
            ag_copy(d, s).start()
        sib_copy(s).start()
        acc[...] += gather(s)
        return c

    lax.fori_loop(1, ring - 1, gather_step, 0)
    for d in range(2):
        ag_copy(d, ring - 2).wait_recv()
    sib_copy(ring - 1).start()
    found = (acc[...] + gather(ring - 1)).astype(BF)
    fine_ref[...] = (hid[...].astype(F32) + dot(found, w_down[...])).astype(BF)

    for l in range(ROUNDS):
        for c in halo(l):
            c.wait_send()
    row_copy.wait_send()
    for i in range(4):
        msg_copy(i).wait_send()

    def drain_counts(j, c):
        count_copy((me + j) % n, me).wait_send()
        return c

    lax.fori_loop(1, n, drain_counts, 0)

    def drain_ring(s, c):
        for d in range(2):
            red_copy(d, s).wait_send()
            ag_copy(d, s).wait_send()
        sib_copy(s).wait_send()
        return c

    lax.fori_loop(0, ring - 1, drain_ring, 0)
    sib_copy(ring - 1).wait_send()


def shards(n, node_feat, coarse_feat, neighbors, up_owner, up_local, *weights):
    rows, width = node_feat.shape
    cells = coarse_feat.shape[0]
    edges = neighbors.shape[1]
    blocks = rows // BLOCK
    window = BLOCK + 2 * R
    ring = n // 2
    half = cells // 2
    parent = up_owner[:, 0] * cells + up_local
    dma = pltpu.SemaphoreType.DMA
    vmem = pl.BlockSpec(memory_space=pltpu.VMEM)
    return pl.pallas_call(
        functools.partial(kernel, n),
        out_shape=(
            jax.ShapeDtypeStruct((rows, width), BF),
            jax.ShapeDtypeStruct((cells, width), BF),
        ),
        in_specs=[vmem] * 14,
        out_specs=(vmem, vmem),
        scratch_shapes=[
            pltpu.VMEM((blocks, edges * BLOCK, window), BF),
            pltpu.VMEM((ROUNDS, rows + 2 * R, width), BF),
            pltpu.VMEM((rows, width), F32),
            pltpu.VMEM((rows, width), BF),
            pltpu.VMEM((rows, width), BF),
            pltpu.VMEM((2, rows, width), BF),
            pltpu.VMEM((1, rows), jnp.int32),
            pltpu.VMEM((8 * n, cells), F32),
            pltpu.VMEM((8 * n, cells), F32),
            pltpu.VMEM((ring - 1, 2, half, width), BF),
            pltpu.VMEM((ring - 1, 2, half, width), BF),
            pltpu.VMEM((2, ring, 2, half, width), BF),
            pltpu.VMEM((rows, width), F32),
            dma((ROUNDS, 2)),
            dma((ROUNDS, 2)),
            dma((n,)),
            dma((n,)),
            dma,
            dma,
            dma((4,)),
            dma((4,)),
            dma((ring - 1, 2)),
            dma((ring - 1, 2)),
            dma((ring - 1, 2)),
            dma((ring - 1, 2)),
            dma((ring,)),
            dma((ring,)),
        ],
        compiler_params=pltpu.CompilerParams(
            collective_id=0, has_side_effects=True, vmem_limit_bytes=48 * 1024 * 1024
        ),
    )(
        node_feat,
        coarse_feat,
        neighbors,
        parent[:, None],
        parent[None, :],
        *weights,
    )


def solution(mesh):
    both = P(("groups", "mesh"), None)
    in_specs = (both, both, P("mesh", None), P("mesh", None), P("mesh")) + (P(),) * 9
    return jax.shard_map(
        functools.partial(shards, mesh.shape["mesh"]),
        mesh=mesh,
        in_specs=in_specs,
        out_specs=(both, both),
        check_vma=False,
    )
```

time: 159 us -> 82.5 us (0.52)
  Pallas kernels: 0 us -> 71 us
  matrix products: 36.9 us -> 0 us
  blocking collectives: 31.8 us -> 0 us
  waiting for transfers between devices: 26.7 us -> 0 us
  starting transfers between devices: 17 us -> 0 us
  other arithmetic: 16.8 us -> 0.7 us
  loops' own time: 10.9 us -> 0 us
  local copies, waits for them, and re-layouts: 16.3 us -> 9.7 us
    pallas_call x0 -> x1, Pallas kernels: none -> 71 us  [shards(): pl.pallas_call(functools.partial(kernel, n), out_shape=(jax.ShapeDtypeStr...]
    dot_general x29 -> x0, matrix products: 36.9 us -> none  [the longest x16 22.6 us: edge_block(): jnp.einsum('cai,iy->cay', indicator_matrix, window_span, preferred_elemen...]
    all_to_all x1 -> x0, blocking collectives: 31.8 us -> none  [shards(): lax.all_to_all(replies.reshape(peer_count, slot_capacity, width), 'mesh',...]
    all_to_all x2 -> x0, waiting for transfers between devices: 22.8 us -> none  [the longest x1 22.8 us: shards(): lax.all_to_all(outbox.reshape(peer_count, slot_capacity, width), 'mesh',...]
    all_to_all x2 -> x0, starting transfers between devices: 12.7 us -> none  [the longest x1 6.46 us: shards(): lax.all_to_all(outbox_index.reshape(peer_count, slot_capacity), 'mesh', s...]
    sub x17 -> x0, other arithmetic: 11.6 us -> none  [the longest x16 11 us: edge_block(): relative_index = index_block - block_start]
    another operation x2 -> x0, loops' own time: 10.9 us -> none  [shards(): lax.map(edge_block, (jnp.arange(number_of_blocks, dtype=jnp.int32), index...]
    unnamed x30 -> x29, local copies, waits for them, and re-layouts: 0.08 us -> 9.48 us
  transfers between devices with their start and end apart: 6 -> 0, of which waited for: 3 -> 0; matrix products, arithmetic and copies ran while one was open for 40% -> 0% of each run, Pallas kernels for 0% -> 0%
where the time goes in v1:
time: 82.5 us; the launch traced here: 82.1 us
  Pallas kernels  71 us (86%)
  local copies, waits for them, and re-layouts  9.7 us (12%)
    pallas_call x1, Pallas kernels, shards(): pl.pallas_call(functools.partial(kernel, n), out_shape=(jax.ShapeDtypeStr...  71 us
    unnamed x29, local copies, waits for them, and re-layouts  9.48 us

profile of v1, /device:TPU:1, one launch (start us, length us, event | category | flops | bytes accessed | tf_op | source)
XLA Modules:
  0.0 82.1 jit_solution(14347026633297081613)
XLA Ops:
  0.6 0.0 copy-start.12
  0.6 0.7 broadcast_multiply_fusion
  1.3 0.0 copy-done.12
  1.3 0.0 copy-start.11
  1.4 0.0 copy-start
  1.4 0.2 copy.18.pc_ref
  1.6 0.5 copy-done.11
  2.1 0.0 copy-start.1
  2.1 0.0 copy-start.2
  2.1 0.0 copy-start.10
  2.1 0.2 copy.17.nb_ref
  2.3 0.1 copy-done
  2.4 0.7 copy-done.1
  3.1 0.1 copy-done.2
  3.2 0.0 copy-done.10
  3.2 0.0 copy-start.3
  3.2 0.9 %copy-done.3 = bf16[2,256,256]{2,1,0:T(8,128)(2,1)S(1)} copy-done((bf16[2,256,256]{2,1,0:T(8,128)(2,1)S(1)}, bf16[2,256,256]{2,1,0:T(8,128)(2,1)}, u32[]{:S(2)}) %copy-start.3) | copy-done | bytes 262168
  4.1 0.0 copy-start.4
  4.1 0.9 %copy-done.4 = bf16[2,256,256]{2,1,0:T(8,128)(2,1)S(1)} copy-done((bf16[2,256,256]{2,1,0:T(8,128)(2,1)S(1)}, bf16[2,256,256]{2,1,0:T(8,128)(2,1)}, u32[]{:S(2)}) %copy-start.4) | copy-done | bytes 262168
  5.1 0.0 copy-start.5
  5.1 0.9 %copy-done.5 = bf16[2,256,256]{2,1,0:T(8,128)(2,1)S(1)} copy-done((bf16[2,256,256]{2,1,0:T(8,128)(2,1)S(1)}, bf16[2,256,256]{2,1,0:T(8,128)(2,1)}, u32[]{:S(2)}) %copy-start.5) | copy-done | bytes 262168
  6.0 0.0 copy-start.6
  6.0 0.9 %copy-done.6 = bf16[256,256]{1,0:T(8,128)(2,1)S(1)} copy-done((bf16[256,256]{1,0:T(8,128)(2,1)S(1)}, bf16[256,256]{1,0:T(8,128)(2,1)}, u32[]{:S(2)}) %copy-start.6) | copy-done | bytes 131096
  6.9 0.0 copy-start.7
  6.9 0.9 %copy-done.7 = bf16[256,256]{1,0:T(8,128)(2,1)S(1)} copy-done((bf16[256,256]{1,0:T(8,128)(2,1)S(1)}, bf16[256,256]{1,0:T(8,128)(2,1)}, u32[]{:S(2)}) %copy-start.7) | copy-done | bytes 131096
  7.8 0.0 copy-start.8
  7.8 0.9 %copy-done.8 = bf16[256,256]{1,0:T(8,128)(2,1)S(1)} copy-done((bf16[256,256]{1,0:T(8,128)(2,1)S(1)}, bf16[256,256]{1,0:T(8,128)(2,1)}, u32[]{:S(2)}) %copy-start.8) | copy-done | bytes 131096
  8.7 0.0 copy-start.9
  8.7 0.9 %copy-done.9 = bf16[256,256]{1,0:T(8,128)(2,1)S(1)} copy-done((bf16[256,256]{1,0:T(8,128)(2,1)S(1)}, bf16[256,256]{1,0:T(8,128)(2,1)}, u32[]{:S(2)}) %copy-start.9) | copy-done | bytes 131096
  9.6 71.0 %shard_map.149 = (bf16[1024,256]{1,0:T(8,128)(2,1)S(1)}, bf16[256,256]{1,0:T(8,128)(2,1)S(1)}) custom-call(bf16[1024,256]{1,0:T(8,128)(2,1)S(1)} %copy-done, bf16[256,256]{1,0:T(8,128)(2,1)S(1)} %copy-done.6, s32[1024,6]{1,0:T(8,128)S(1)} %copy.17.nb_ref, s32[1024,1]{1,0:T(8,128)S(1)} %copy.18.pc_ref, s32[1,1024]{1,0:T(1,128)S(1)} %bitcast.4, ...), custom_call_target="tpu_custom_call" | custom-call | tf_op jit(solution)/shard_map/pallas_call | solution.py:378
  80.7 0.8 copy.21
  81.4 0.7 copy.22
  (1 shorter events, 0.0 us)
Async XLA Ops:
  0.6 0.7 copy-start.12
  1.3 0.8 copy-start.11
  1.4 1.0 %copy-start = (bf16[1024,256]{1,0:T(8,128)(2,1)S(1)}, bf16[1024,256]{1,0:T(8,128)(2,1)}, u32[]{:S(2)}) copy-start(bf16[1024,256]{1,0:T(8,128)(2,1)} %x_ref.1) | copy-start | bytes 1572868
  2.1 1.0 %copy-start.1 = (bf16[2,256,256]{2,1,0:T(8,128)(2,1)S(1)}, bf16[2,256,256]{2,1,0:T(8,128)(2,1)}, u32[]{:S(2)}) copy-start(bf16[2,256,256]{2,1,0:T(8,128)(2,1)} %w_src.1) | copy-start | bytes 786436
  2.1 1.1 %copy-start.2 = (bf16[2,256,256]{2,1,0:T(8,128)(2,1)S(1)}, bf16[2,256,256]{2,1,0:T(8,128)(2,1)}, u32[]{:S(2)}) copy-start(bf16[2,256,256]{2,1,0:T(8,128)(2,1)} %w_dst.1) | copy-start | bytes 786436
  2.1 1.1 %copy-start.10 = (f32[2,256]{1,0:T(2,128)S(1)}, f32[2,256]{1,0:T(2,128)}, u32[]{:S(2)}) copy-start(f32[2,256]{1,0:T(2,128)} %bias_ref.1) | copy-start | bytes 6148
  3.2 1.0 %copy-start.3 = (bf16[2,256,256]{2,1,0:T(8,128)(2,1)S(1)}, bf16[2,256,256]{2,1,0:T(8,128)(2,1)}, u32[]{:S(2)}) copy-start(bf16[2,256,256]{2,1,0:T(8,128)(2,1)} %w_node.1) | copy-start | bytes 786436
  4.1 0.9 %copy-start.4 = (bf16[2,256,256]{2,1,0:T(8,128)(2,1)S(1)}, bf16[2,256,256]{2,1,0:T(8,128)(2,1)}, u32[]{:S(2)}) copy-start(bf16[2,256,256]{2,1,0:T(8,128)(2,1)} %w_edge.1) | copy-start | bytes 786436
  5.1 0.9 %copy-start.5 = (bf16[2,256,256]{2,1,0:T(8,128)(2,1)S(1)}, bf16[2,256,256]{2,1,0:T(8,128)(2,1)}, u32[]{:S(2)}) copy-start(bf16[2,256,256]{2,1,0:T(8,128)(2,1)} %w_mix.1) | copy-start | bytes 786436
  6.0 0.9 %copy-start.6 = (bf16[256,256]{1,0:T(8,128)(2,1)S(1)}, bf16[256,256]{1,0:T(8,128)(2,1)}, u32[]{:S(2)}) copy-start(bf16[256,256]{1,0:T(8,128)(2,1)} %cf_ref.1) | copy-start | bytes 393220
  6.9 0.9 %copy-start.7 = (bf16[256,256]{1,0:T(8,128)(2,1)S(1)}, bf16[256,256]{1,0:T(8,128)(2,1)}, u32[]{:S(2)}) copy-start(bf16[256,256]{1,0:T(8,128)(2,1)} %w_up.1) | copy-start | bytes 393220
  7.8 0.9 %copy-start.8 = (bf16[256,256]{1,0:T(8,128)(2,1)S(1)}, bf16[256,256]{1,0:T(8,128)(2,1)}, u32[]{:S(2)}) copy-start(bf16[256,256]{1,0:T(8,128)(2,1)} %w_coarse.1) | copy-start | bytes 393220
  8.7 0.9 %copy-start.9 = (bf16[256,256]{1,0:T(8,128)(2,1)S(1)}, bf16[256,256]{1,0:T(8,128)(2,1)}, u32[]{:S(2)}) copy-start(bf16[256,256]{1,0:T(8,128)(2,1)} %w_down.1) | copy-start | bytes 393220

commit v2 on v1

--- a/solution.py
+++ b/solution.py
@@ -10,6 +10,7 @@
 R = 128
 ROUNDS = 2
 BLOCK = 128
+LOAD_ORDER = (0, 4, 3, 2, 8, 5, 6, 7, 9, 1, 10, 11)
 BF = jnp.bfloat16
 F32 = jnp.float32
 
@@ -25,11 +26,23 @@
 
 def kernel(
     n,
+    pc_ref,
+    pr_ref,
+    *refs,
+):
+    given, (fine_ref, coarse_ref), held = refs[:12], refs[12:14], refs[14:26]
+    sweep(n, pc_ref, pr_ref, given, held, *held, fine_ref, coarse_ref, *refs[26:])
+
+
+def sweep(
+    n,
+    pc_ref,
+    pr_ref,
+    given,
+    held,
     x_ref,
     cf_ref,
     nb_ref,
-    pc_ref,
-    pr_ref,
     w_src,
     w_dst,
     w_node,
@@ -41,6 +54,7 @@
     w_down,
     fine_ref,
     coarse_ref,
+    load_s,
     pick,
     ext,
     srch,
@@ -114,7 +128,12 @@
         )
         return c
 
+    loads = [pltpu.make_async_copy(a, b, load_s.at[i]) for i, (a, b) in enumerate(zip(given, held))]
+    for i in LOAD_ORDER:
+        loads[i].start()
     lax.fori_loop(1, n, greet, 0)
+    for i in LOAD_ORDER:
+        loads[i].wait()
 
     ext[0, pl.ds(R, rows), :] = dot(x_ref[...], w_dst[0]).astype(BF)
     lows = (lax.broadcasted_iota(jnp.int32, (8 * n, 1), 0) // 8) * cells
@@ -125,6 +144,45 @@
         local == lax.broadcasted_iota(jnp.int32, (rows, cells), 1), 1.0, 0.0
     ).astype(BF)
     hist[...] = dot(owner_hot, local_hot)
+
+    def build(b, c):
+        r0 = b * BLOCK
+        rel = nb_ref[pl.ds(r0, BLOCK), :] - (me * rows - R)
+        rel = jnp.where(rel < 0, rel + total, rel)
+        rel = jnp.where(rel >= total, rel - total, rel) - r0
+        lanes = lax.broadcasted_iota(jnp.int32, (BLOCK, window), 1)
+        for k in range(edges):
+            pick[b, pl.ds(k * BLOCK, BLOCK), :] = jnp.where(
+                rel[:, k : k + 1] == lanes, 0.5, 0.0
+            ).astype(BF)
+        return c
+
+    def edge_block(l, b):
+        r0 = b * BLOCK
+        if l == 0:
+            build(b, 0)
+        sel = dot(pick[b], ext[l, pl.ds(r0, window), :])
+        base = srch[pl.ds(r0, BLOCK), :]
+        out = jnp.zeros((BLOCK, width), F32)
+        for k in range(edges):
+            h = base + sel[k * BLOCK : (k + 1) * BLOCK]
+            out = out + (h + h * jnp.tanh(h))
+        esum[pl.ds(r0, BLOCK), :] = out.astype(BF)
+
+    def inner(l, low, high):
+        def step(b, c):
+            edge_block(l, b)
+            return c
+
+        lax.fori_loop(low, high, step, 0)
+
+    def src_terms(l):
+        here = x_ref if l == 0 else hid
+        srch[...] = 0.5 * (dot(here[...], w_src[l]) + bias_ref[l : l + 1, :])
+
+    early = 1 + (blocks - 2) // 2
+    src_terms(0)
+    inner(0, 1, early)
 
     pl.semaphore_wait(barrier, n - 1)
 
@@ -166,30 +224,6 @@
 
     lax.fori_loop(1, n, send_counts, 0)
 
-    def build(b, c):
-        r0 = b * BLOCK
-        rel = nb_ref[pl.ds(r0, BLOCK), :] - (me * rows - R)
-        rel = jnp.where(rel < 0, rel + total, rel)
-        rel = jnp.where(rel >= total, rel - total, rel) - r0
-        lanes = lax.broadcasted_iota(jnp.int32, (BLOCK, window), 1)
-        for k in range(edges):
-            pick[b, pl.ds(k * BLOCK, BLOCK), :] = jnp.where(
-                rel[:, k : k + 1] == lanes, 0.5, 0.0
-            ).astype(BF)
-        return c
-
-    def edge_block(l, b):
-        r0 = b * BLOCK
-        if l == 0:
-            build(b, 0)
-        sel = dot(pick[b], ext[l, pl.ds(r0, window), :])
-        base = srch[pl.ds(r0, BLOCK), :]
-        out = jnp.zeros((BLOCK, width), F32)
-        for k in range(edges):
-            h = base + sel[k * BLOCK : (k + 1) * BLOCK]
-            out = out + (h + h * jnp.tanh(h))
-        esum[pl.ds(r0, BLOCK), :] = out.astype(BF)
-
     chunk = rows // 4
 
     def msg_copy(i):
@@ -198,13 +232,11 @@
 
     for l in range(ROUNDS):
         here = x_ref if l == 0 else hid
-        srch[...] = 0.5 * (dot(here[...], w_src[l]) + bias_ref[l : l + 1, :])
-
-        def inner(b, c, l=l):
-            edge_block(l, b)
-            return c
-
-        lax.fori_loop(1, blocks - 1, inner, 0)
+        if l == 0:
+            inner(0, early, blocks - 1)
+        else:
+            src_terms(l)
+            inner(l, 1, blocks - 1)
         for c in halo(l):
             c.wait_recv()
 
@@ -248,96 +280,111 @@
     for i in range(4):
         msg_copy(i).wait_recv()
 
+    far = ring // 2
     cell_iota = lax.broadcasted_iota(jnp.int32, (cells, 1), 0)
-
-    def partial_sums(s):
-        low = (owner_at(pos - 1 - s) + core) * cells
-        high = (owner_at(pos + 1 + s) + core) * cells
-        ids = cell_iota + jnp.where(cell_iota < half, low, high)
+    parts = (slice(0, half), slice(half, cells))
+
+    def partial_sums(place):
+        ids = cell_iota + (owner_at(place) + core) * cells
         mine = jnp.where(pr_ref[...] == ids, 1.0, 0.0).astype(BF)
         theirs = jnp.where(sib_row[...] == ids, 1.0, 0.0).astype(BF)
         return dot(mine, msg[0]) + dot(theirs, msg[1])
 
-    def red_copy(d, s):
+    def red_copy(d, h, s):
         return remote(
-            sbuf.at[s, d],
-            rbuf.at[s, d],
-            red_s.at[s, d],
-            red_r.at[s, d],
+            sbuf.at[s, d, h],
+            rbuf.at[s, d, h],
+            red_s.at[s, d, h],
+            red_r.at[s, d, h],
             right if d == 0 else left,
         )
 
-    first = partial_sums(0)
+    def reduce_step(s, first):
+        own = (partial_sums(pos + (far - s)), partial_sums(pos - (far - s)))
+        pieces = ((0, 1), (1, 0), (0, 0), (1, 1))
+        for d, h in pieces:
+            part = own[d][parts[h]]
+            if not (first and d != h):
+                red_copy(d, h, s - 1).wait_recv()
+                part = part + rbuf[s - 1, d, h].astype(F32)
+            sbuf[s, d, h] = part.astype(BF)
+            red_copy(d, h, s).start()
+
+    part = partial_sums(pos + far)
     for d in range(2):
-        sbuf[0, d] = first[d * half : (d + 1) * half].astype(BF)
-        red_copy(d, 0).start()
-
-    def reduce_step(s, c):
-        part = partial_sums(s)
+        sbuf[0, d, d] = part[parts[d]].astype(BF)
+        red_copy(d, d, 0).start()
+    reduce_step(1, True)
+
+    def reduce_loop(s, c):
+        reduce_step(s, False)
+        return c
+
+    lax.fori_loop(2, far, reduce_loop, 0)
+    part = partial_sums(pos)
+
+    def ag_copy(d, h, s, last=False):
+        return remote(
+            gath.at[0, s, d, h],
+            gath.at[0, s + 1, 0 if last else d, h],
+            ag_s.at[s, d, h],
+            ag_r.at[s, d, h],
+            right if d == 0 else left,
+        )
+
+    def sib_copy(s, d):
+        return remote(gath.at[0, s, d], gath.at[1, s, d], sib_s.at[s, d], sib_r.at[s, d], sibling)
+
+    for h in (1, 0):
+        summed = part[parts[h]]
         for d in range(2):
-            red_copy(d, s - 1).wait_recv()
-            sbuf[s, d] = (
-                part[d * half : (d + 1) * half] + rbuf[s - 1, d].astype(F32)
-            ).astype(BF)
-            red_copy(d, s).start()
-        return c
-
-    lax.fori_loop(1, ring - 1, reduce_step, 0)
-    part = partial_sums(ring - 1)
+            red_copy(d, h, far - 1).wait_recv()
+            summed = summed + rbuf[far - 1, d, h].astype(F32)
+        mean = (summed * scale[parts[h]]).astype(BF)
+        out = (cf_ref[parts[h], :].astype(F32) + dot(mean, w_coarse[...])).astype(BF)
+        gath[0, 0, 0, h] = out
+        gath[0, 0, 1, h] = out
+        ag_copy(0, h, 0).start()
+        ag_copy(1, h, 0).start()
+        coarse_ref[parts[h], :] = out
+    sib_copy(0, 0).start()
+
+    lane_iota = lax.broadcasted_iota(jnp.int32, (1, cells), 1)
+
+    def gather(s, d, slot):
+        owner = owner_at(pos - s if d == 0 else pos + s) + (core if slot == 0 else 1 - core)
+        hot = jnp.where(pc_ref[...] == lane_iota + owner * cells, 1.0, 0.0).astype(BF)
+        return dot(hot, gath[slot, s, d].reshape(cells, width))
+
+    acc[...] = gather(0, 0, 0)
+    sib_copy(0, 0).wait_recv()
+    acc[...] += gather(0, 0, 1)
+
+    def gather_step(s, last):
+        for h in (1, 0):
+            for d in range(2):
+                ag_copy(d, h, s - 1).wait_recv()
+                if not last or d == h:
+                    ag_copy(d, h, s, last).start()
+        for d in range(2):
+            sib_copy(s, d).start()
+        acc[...] += gather(s, 0, 0) + gather(s, 1, 0)
+        for d in range(2):
+            sib_copy(s, d).wait_recv()
+        acc[...] += gather(s, 0, 1) + gather(s, 1, 1)
+
+    def gather_loop(s, c):
+        gather_step(s, False)
+        return c
+
+    lax.fori_loop(1, far - 1, gather_loop, 0)
+    gather_step(far - 1, True)
     for d in range(2):
-        red_copy(d, ring - 2).wait_recv()
-        side = slice(d * half, (d + 1) * half)
-        summed = part[side] + rbuf[ring - 2, d].astype(F32)
-        mean = (summed * scale[side]).astype(BF)
-        out = (cf_ref[side, :].astype(F32) + dot(mean, w_coarse[...])).astype(BF)
-        coarse_ref[side, :] = out
-        gath[0, 0, d] = out
-
-    def ag_copy(d, s):
-        return remote(
-            gath.at[0, s, d],
-            gath.at[0, s + 1, d],
-            ag_s.at[s, d],
-            ag_r.at[s, d],
-            right if d == 0 else left,
-        )
-
-    def sib_copy(s):
-        return remote(gath.at[0, s], gath.at[1, s], sib_s.at[s], sib_r.at[s], sibling)
-
-    lane_iota = lax.broadcasted_iota(jnp.int32, (1, cells), 1)
-
-    def gather(s):
-        low = owner_at(pos - s)
-        high = owner_at(pos + s)
-        ids = lane_iota + jnp.where(lane_iota < half, low, high) * cells
-        mine = ids + core * cells
-        theirs = ids + (1 - core) * cells
-        column = pc_ref[...]
-        hot = jnp.where(column == mine, 1.0, 0.0).astype(BF)
-        got = dot(hot, gath[0, s].reshape(cells, width))
-        sib_copy(s).wait_recv()
-        hot = jnp.where(column == theirs, 1.0, 0.0).astype(BF)
-        return got + dot(hot, gath[1, s].reshape(cells, width))
-
-    for d in range(2):
-        ag_copy(d, 0).start()
-    sib_copy(0).start()
-    acc[...] = gather(0)
-
-    def gather_step(s, c):
-        for d in range(2):
-            ag_copy(d, s - 1).wait_recv()
-            ag_copy(d, s).start()
-        sib_copy(s).start()
-        acc[...] += gather(s)
-        return c
-
-    lax.fori_loop(1, ring - 1, gather_step, 0)
-    for d in range(2):
-        ag_copy(d, ring - 2).wait_recv()
-    sib_copy(ring - 1).start()
-    found = (acc[...] + gather(ring - 1)).astype(BF)
+        ag_copy(d, d, far - 1, True).wait_recv()
+    sib_copy(far, 0).start()
+    acc[...] += gather(far, 0, 0)
+    sib_copy(far, 0).wait_recv()
+    found = (acc[...] + gather(far, 0, 1)).astype(BF)
     fine_ref[...] = (hid[...].astype(F32) + dot(found, w_down[...])).astype(BF)
 
     for l in range(ROUNDS):
@@ -353,15 +400,21 @@
 
     lax.fori_loop(1, n, drain_counts, 0)
 
+    for d in range(2):
+        red_copy(d, d, 0).wait_send()
+        ag_copy(d, d, far - 1, True).wait_send()
+    sib_copy(0, 0).wait_send()
+    sib_copy(far, 0).wait_send()
+
     def drain_ring(s, c):
         for d in range(2):
-            red_copy(d, s).wait_send()
-            ag_copy(d, s).wait_send()
-        sib_copy(s).wait_send()
-        return c
-
-    lax.fori_loop(0, ring - 1, drain_ring, 0)
-    sib_copy(ring - 1).wait_send()
+            for h in range(2):
+                red_copy(d, h, s).wait_send()
+                ag_copy(d, h, s - 1).wait_send()
+            sib_copy(s, d).wait_send()
+        return c
+
+    lax.fori_loop(1, far, drain_ring, 0)
 
 
 def shards(n, node_feat, coarse_feat, neighbors, up_owner, up_local, *weights):
@@ -370,8 +423,9 @@
     edges = neighbors.shape[1]
     blocks = rows // BLOCK
     window = BLOCK + 2 * R
-    ring = n // 2
+    far = n // 4
     half = cells // 2
+    operands = (node_feat, coarse_feat, neighbors) + weights
     parent = up_owner[:, 0] * cells + up_local
     dma = pltpu.SemaphoreType.DMA
     vmem = pl.BlockSpec(memory_space=pltpu.VMEM)
@@ -381,9 +435,11 @@
             jax.ShapeDtypeStruct((rows, width), BF),
             jax.ShapeDtypeStruct((cells, width), BF),
         ),
-        in_specs=[vmem] * 14,
+        in_specs=[vmem] * 2 + [pl.BlockSpec(memory_space=pl.ANY)] * 12,
         out_specs=(vmem, vmem),
-        scratch_shapes=[
+        scratch_shapes=[pltpu.VMEM(a.shape, a.dtype) for a in operands]
+        + [
+            dma((len(operands),)),
             pltpu.VMEM((blocks, edges * BLOCK, window), BF),
             pltpu.VMEM((ROUNDS, rows + 2 * R, width), BF),
             pltpu.VMEM((rows, width), F32),
@@ -393,9 +449,9 @@
             pltpu.VMEM((1, rows), jnp.int32),
             pltpu.VMEM((8 * n, cells), F32),
             pltpu.VMEM((8 * n, cells), F32),
-            pltpu.VMEM((ring - 1, 2, half, width), BF),
-            pltpu.VMEM((ring - 1, 2, half, width), BF),
-            pltpu.VMEM((2, ring, 2, half, width), BF),
+            pltpu.VMEM((far, 2, 2, half, width), BF),
+            pltpu.VMEM((far, 2, 2, half, width), BF),
+            pltpu.VMEM((2, far + 1, 2, 2, half, width), BF),
             pltpu.VMEM((rows, width), F32),
             dma((ROUNDS, 2)),
             dma((ROUNDS, 2)),
@@ -405,23 +461,20 @@
             dma,
             dma((4,)),
             dma((4,)),
-            dma((ring - 1, 2)),
-            dma((ring - 1, 2)),
-            dma((ring - 1, 2)),
-            dma((ring - 1, 2)),
-            dma((ring,)),
-            dma((ring,)),
+            dma((far, 2, 2)),
+            dma((far, 2, 2)),
+            dma((far, 2, 2)),
+            dma((far, 2, 2)),
+            dma((far + 1, 2)),
+            dma((far + 1, 2)),
         ],
         compiler_params=pltpu.CompilerParams(
-            collective_id=0, has_side_effects=True, vmem_limit_bytes=48 * 1024 * 1024
+            collective_id=0, has_side_effects=True, vmem_limit_bytes=60 * 1024 * 1024
         ),
     )(
-        node_feat,
-        coarse_feat,
-        neighbors,
         parent[:, None],
         parent[None, :],
-        *weights,
+        *operands,
     )
 
 

time: 82.5 us -> 61.1 us (0.74)
  Pallas kernels: 71 us -> 54.9 us
  local copies, waits for them, and re-layouts: 9.7 us -> 4.64 us
    pallas_call x1, Pallas kernels: 71 us -> 54.9 us  [shards(): pl.pallas_call(functools.partial(kernel, n), out_shape=(jax.ShapeDtypeStr...]
    unnamed x29 -> x11, local copies, waits for them, and re-layouts: 9.48 us -> 3.61 us
where the time goes in v2:
time: 61.1 us; the launch traced here: 60.9 us
  Pallas kernels  54.9 us (90%)
  local copies, waits for them, and re-layouts  4.64 us (8%)
  other arithmetic  0.7 us (1%)
  between operations  0.68 us (1%)
    pallas_call x1, Pallas kernels, shards(): pl.pallas_call(functools.partial(kernel, n), out_shape=(jax.ShapeDtypeStr...  54.9 us
    unnamed x11, local copies, waits for them, and re-layouts  3.61 us

profile of v2, /device:TPU:1, one launch (start us, length us, event | category | flops | bytes accessed | tf_op | source)
XLA Modules:
  0.0 60.9 jit_solution(660451569393101649)
XLA Ops:
  0.6 0.0 copy-start.3
  0.6 0.7 %broadcast_multiply_fusion = s32[1024,1]{0,1:T(1,128)S(1)} fusion(s32[1024,1]{0,1:T(1,128)} %param.17), kind=kLoop, calls=%fused_computation | loop fusion | flops 1024 | bytes 8192 | tf_op jit(solution)/shard_map/mul | solution.py:429
  1.3 0.0 copy-done.3
  1.3 0.0 copy-start.1
  1.4 0.0 copy-start.2
  1.4 1.0 %copy.17.pc_ref = s32[1024,1]{1,0:T(8,128)} copy(s32[1024,1]{0,1:T(1,128)S(1)} %bitcast.3) | data formatting | bytes 8192 | tf_op jit(solution)/shard_map/broadcast_in_dim | solution.py:475
  2.4 0.0 copy-done.1
  2.4 0.0 copy-done.2
  2.4 1.0 %copy.18.refs_2_ = s32[1024,6]{1,0:T(8,128)} copy(s32[1024,6]{0,1:T(8,128)S(1)} %copy-done.2) | data formatting | bytes 49152 | tf_op args[2]
  3.4 54.9 %shard_map.149 = (bf16[1024,256]{1,0:T(8,128)(2,1)}, bf16[256,256]{1,0:T(8,128)(2,1)}) custom-call(s32[1024,1]{1,0:T(8,128)} %copy.17.pc_ref, s32[1,1024]{1,0:T(1,128)} %bitcast.4, bf16[1024,256]{1,0:T(8,128)(2,1)} %refs_0_.1, bf16[256,256]{1,0:T(8,128)(2,1)} %refs_1_.1, s32[1024,6]{1,0:T(8,128)} %copy.18.refs_2_, bf16[2,256,256]{2,1,0:T(8,128)(2,1)} %refs_3_.1, ...), custom_call_target="tpu_custom_call" | custom-call | tf_op jit(solution)/shard_map/pallas_call | solution.py:432
  58.4 0.0 copy-start
  58.4 1.9 %copy.21 = bf16[1024,256]{1,0:T(8,128)(2,1)} copy(bf16[1024,256]{1,0:T(8,128)(2,1)} %get-tuple-element.4) | data formatting | bytes 1048576
  60.3 0.0 copy-done
  60.3 0.7 %copy.22 = bf16[256,256]{1,0:T(8,128)(2,1)} copy(bf16[256,256]{1,0:T(8,128)(2,1)S(1)} %copy-done) | data formatting | bytes 262144
  (1 shorter events, 0.0 us)
Async XLA Ops:
  0.6 0.7 %copy-start.3 = (s32[1024]{0:T(1024)S(1)}, s32[1024]{0:T(1024)}, u32[]{:S(2)}) copy-start(s32[1024]{0:T(1024)} %param.18) | copy-start | bytes 12292
  1.3 1.1 %copy-start.1 = (s32[1024]{0:T(1024)}, s32[1024]{0:T(1024)S(1)}, u32[]{:S(2)}) copy-start(s32[1024]{0:T(1024)S(1)} %add.3) | copy-start | bytes 12292
  1.4 1.0 %copy-start.2 = (s32[1024,6]{0,1:T(8,128)S(1)}, s32[1024,6]{0,1:T(8,128)}, u32[]{:S(2)}) copy-start(s32[1024,6]{0,1:T(8,128)} %param.16) | copy-start | bytes 73732
  58.4 1.9 %copy-start = (bf16[256,256]{1,0:T(8,128)(2,1)S(1)}, bf16[256,256]{1,0:T(8,128)(2,1)}, u32[]{:S(2)}) copy-start(bf16[256,256]{1,0:T(8,128)(2,1)} %get-tuple-element.5) | copy-start | bytes 393220

commit v3 on v2

--- a/solution.py
+++ b/solution.py
@@ -26,18 +26,18 @@
 
 def kernel(
     n,
-    pc_ref,
-    pr_ref,
+    own_ref,
+    loc_ref,
     *refs,
 ):
     given, (fine_ref, coarse_ref), held = refs[:12], refs[12:14], refs[14:26]
-    sweep(n, pc_ref, pr_ref, given, held, *held, fine_ref, coarse_ref, *refs[26:])
+    sweep(n, own_ref, loc_ref, given, held, *held, fine_ref, coarse_ref, *refs[26:])
 
 
 def sweep(
     n,
-    pc_ref,
-    pr_ref,
+    own_ref,
+    loc_ref,
     given,
     held,
     x_ref,
@@ -55,6 +55,8 @@
     fine_ref,
     coarse_ref,
     load_s,
+    pr_ref,
+    pc_ref,
     pick,
     ext,
     srch,
@@ -84,7 +86,7 @@
     sib_r,
 ):
     rows, width = x_ref.shape
-    edges = nb_ref.shape[1]
+    edges = nb_ref.shape[0]
     cells = cf_ref.shape[0]
     half = cells // 2
     blocks = rows // BLOCK
@@ -136,6 +138,19 @@
         loads[i].wait()
 
     ext[0, pl.ds(R, rows), :] = dot(x_ref[...], w_dst[0]).astype(BF)
+    square = lax.broadcasted_iota(jnp.int32, (BLOCK, BLOCK), 0) == lax.broadcasted_iota(
+        jnp.int32, (BLOCK, BLOCK), 1
+    )
+
+    def upright(row):
+        return jnp.sum(jnp.where(square, row.astype(F32), 0.0), axis=1, keepdims=True).astype(
+            jnp.int32
+        )
+
+    pr_ref[...] = own_ref[...] * cells + loc_ref[...]
+    for b in range(blocks):
+        part = slice(b * BLOCK, (b + 1) * BLOCK)
+        pc_ref[part, :] = upright(pr_ref[:, part])
     lows = (lax.broadcasted_iota(jnp.int32, (8 * n, 1), 0) // 8) * cells
     parents = pr_ref[...]
     owner_hot = jnp.where((parents >= lows) & (parents < lows + cells), 1.0, 0.0).astype(BF)
@@ -147,13 +162,13 @@
 
     def build(b, c):
         r0 = b * BLOCK
-        rel = nb_ref[pl.ds(r0, BLOCK), :] - (me * rows - R)
+        rel = nb_ref[:, pl.ds(pl.multiple_of(r0, BLOCK), BLOCK)] - (me * rows - R)
         rel = jnp.where(rel < 0, rel + total, rel)
         rel = jnp.where(rel >= total, rel - total, rel) - r0
         lanes = lax.broadcasted_iota(jnp.int32, (BLOCK, window), 1)
         for k in range(edges):
             pick[b, pl.ds(k * BLOCK, BLOCK), :] = jnp.where(
-                rel[:, k : k + 1] == lanes, 0.5, 0.0
+                upright(rel[k : k + 1, :]) == lanes, 0.5, 0.0
             ).astype(BF)
         return c
 
@@ -180,7 +195,7 @@
         here = x_ref if l == 0 else hid
         srch[...] = 0.5 * (dot(here[...], w_src[l]) + bias_ref[l : l + 1, :])
 
-    early = 1 + (blocks - 2) // 2
+    early = blocks - 1 - (blocks - 2) // 6
     src_terms(0)
     inner(0, 1, early)
 
@@ -425,8 +440,7 @@
     window = BLOCK + 2 * R
     far = n // 4
     half = cells // 2
-    operands = (node_feat, coarse_feat, neighbors) + weights
-    parent = up_owner[:, 0] * cells + up_local
+    operands = (node_feat, coarse_feat, neighbors.T) + weights
     dma = pltpu.SemaphoreType.DMA
     vmem = pl.BlockSpec(memory_space=pltpu.VMEM)
     return pl.pallas_call(
@@ -440,6 +454,8 @@
         scratch_shapes=[pltpu.VMEM(a.shape, a.dtype) for a in operands]
         + [
             dma((len(operands),)),
+            pltpu.VMEM((1, rows), jnp.int32),
+            pltpu.VMEM((rows, 1), jnp.int32),
             pltpu.VMEM((blocks, edges * BLOCK, window), BF),
             pltpu.VMEM((ROUNDS, rows + 2 * R, width), BF),
             pltpu.VMEM((rows, width), F32),
@@ -472,8 +488,8 @@
             collective_id=0, has_side_effects=True, vmem_limit_bytes=60 * 1024 * 1024
         ),
     )(
-        parent[:, None],
-        parent[None, :],
+        up_owner.reshape(1, rows),
+        up_local.reshape(1, rows),
         *operands,
     )
 

time: 61.1 us -> 59.4 us (0.972)
  local copies, waits for them, and re-layouts: 4.64 us -> 2.56 us
  Pallas kernels: 54.9 us -> 55.9 us
  other arithmetic: 0.7 us -> 0 us
    unnamed x11 -> x4, local copies, waits for them, and re-layouts: 3.61 us -> 2.56 us
    broadcast_in_dim x1 -> x0, local copies, waits for them, and re-layouts: 1.03 us -> none  [shards(): parent[:, None]]
    pallas_call x1, Pallas kernels: 54.9 us -> 55.9 us  [shards(): pl.pallas_call(functools.partial(kernel, n), out_shape=(jax.ShapeDtypeStr...]
    mul x1 -> x0, other arithmetic: 0.7 us -> none  [shards(): parent = up_owner[:, 0] * cells + up_local]
where the time goes in v3:
time: 59.4 us; the launch traced here: 59.1 us
  Pallas kernels  55.9 us (94%)
  local copies, waits for them, and re-layouts  2.56 us (4%)
  between operations  0.65 us (1%)
    pallas_call x1, Pallas kernels, shards(): pl.pallas_call(functools.partial(kernel, n), out_shape=(jax.ShapeDtypeStr...  55.9 us
    unnamed x4, local copies, waits for them, and re-layouts  2.56 us

profile of v3, /device:TPU:1, one launch (start us, length us, event | category | flops | bytes accessed | tf_op | source)
XLA Modules:
  0.0 59.1 jit_solution(17691317267886415117)
XLA Ops:
  0.6 55.9 %shard_map.149 = (bf16[1024,256]{1,0:T(8,128)(2,1)}, bf16[256,256]{1,0:T(8,128)(2,1)}) custom-call(s32[1,1024]{1,0:T(1,128)} %bitcast.4, s32[1,1024]{1,0:T(1,128)} %bitcast.5, bf16[1024,256]{1,0:T(8,128)(2,1)} %refs_0_.1, bf16[256,256]{1,0:T(8,128)(2,1)} %refs_1_.1, s32[6,1024]{1,0:T(8,128)} %bitcast.3, bf16[2,256,256]{2,1,0:T(8,128)(2,1)} %refs_3_.1, ...), custom_call_target="tpu_custom_call" | custom-call | tf_op jit(solution)/shard_map/pallas_call | solution.py:446
  56.6 0.0 copy-start
  56.6 1.9 %copy.18 = bf16[1024,256]{1,0:T(8,128)(2,1)} copy(bf16[1024,256]{1,0:T(8,128)(2,1)} %get-tuple-element.4) | data formatting | bytes 1048576
  58.5 0.0 copy-done
  58.5 0.7 %copy.19 = bf16[256,256]{1,0:T(8,128)(2,1)} copy(bf16[256,256]{1,0:T(8,128)(2,1)S(1)} %copy-done) | data formatting | bytes 262144
Async XLA Ops:
  56.6 1.9 %copy-start = (bf16[256,256]{1,0:T(8,128)(2,1)S(1)}, bf16[256,256]{1,0:T(8,128)(2,1)}, u32[]{:S(2)}) copy-start(bf16[256,256]{1,0:T(8,128)(2,1)} %get-tuple-element.5) | copy-start | bytes 393220
